TPU v7x, 32 devices: a whole 2x2x4 slice. The times are simulated.
32 devices in a mesh: group: 2 (over y), layout: 4 (over z), kernel: 4 (over x, core).
Axes of the slice: x: 2, y: 2, z: 4, core: 2. Of those that a mesh axis runs over, the one named last changes fastest.
Arguments:
- theta: bfloat16 [2048, 512], P(('group', 'layout')), parts along dimension 0, may hold values from -6 to 6
- target: bfloat16 [2048, 512], P(('group', 'layout')), parts along dimension 0, may hold values from 0 to 1
- occupancy: int32 [8, 2], P(('group', 'layout')), parts along dimension 0, may hold values from 0 to 1, as said below
- kernels: bfloat16 [2, 8, 19, 19], P(None, 'kernel'), may hold values from -0.3125 to 0.3125
- kernel_weights: float32 [8], P('kernel'), may hold values from 0.04 to 0.4
Outputs:
- mask_gradient: float32 [2048, 512], P(('group', 'layout', 'kernel')), parts along dimension 0
There are 2 independent parts, one for each index of `group`. A program takes and returns all parts, laid end to end along the dimension named above; an argument that names none is the same for every part. Nothing has to cross between parts.
Inputs may be any that keep to these rules, and one draw needn't show every extreme that they name: `occupancy`: 1 marks a tile that holds layout, 0 an empty tile; exactly 4 tiles of the map are marked 1.
All inputs are finite; a program needn't handle non-finite values.
Results may differ from a plain program's by a relative error of at most 0.0065.
Values may be sent and summed in bfloat16 or wider, within the bound.
A program may use at most 128 MiB of HBM per device.

v0:
```python
import functools
import jax
import jax.numpy as jnp
from jax import lax
from jax.experimental import pallas as pl
from jax.experimental.pallas import tpu as pltpu
from jax.sharding import PartitionSpec as P

steepness = 8.0
threshold = 1.0
step_rows = 16
margin = 16
halo_rows = 32
tap_rows = 24
mesh_id = pl.DeviceIdType.MESH


def band_kernel(
    layouts, sharers, theta_ref, target_ref, occupancy_ref, kernels_ref, weights_ref, out_ref,
    gathered, halo_out, halo_in, mask_ref, target_near, live_near, shifted, products, forward_ref,
    adjoint_ref, send_sem, recv_sem, halo_send_sem, halo_recv_sem,
):
    local_rows, cols = theta_ref.shape
    parts, own_kernels, edge, _ = kernels_ref.shape
    own_channels = parts * own_kernels
    channels = own_channels * sharers
    radius = edge // 2
    share = local_rows // sharers
    lanes = mask_ref.shape[1]
    forward_window = (shifted.shape[1] - (share + 2 * margin)) + step_rows
    forward_depth = forward_ref.shape[1]
    adjoint_window = step_rows + 2 * margin
    adjoint_depth = adjoint_ref.shape[1]
    column = lax.axis_index("layout")
    sharer = lax.axis_index("kernel")
    is_first = sharer == 0
    is_last = sharer == sharers - 1
    has_low = jnp.logical_and(is_first, column > 0)
    has_high = jnp.logical_and(is_last, column < layouts - 1)
    sends_up = jnp.logical_and(is_first, column < layouts - 1)
    sends_down = jnp.logical_and(is_last, column > 0)
    at_edge = jnp.logical_or(is_first, is_last)

    barrier = pltpu.get_barrier_semaphore()
    for offset in range(1, sharers):
        pl.semaphore_signal(
            barrier, inc=1, device_id={"kernel": lax.rem(sharer + offset, sharers)},
            device_id_type=mesh_id,
        )

    @pl.when(jnp.logical_and(at_edge, column > 0))
    def _():
        pl.semaphore_signal(
            barrier, inc=1, device_id={"layout": column - 1}, device_id_type=mesh_id
        )

    @pl.when(jnp.logical_and(at_edge, column < layouts - 1))
    def _():
        pl.semaphore_signal(
            barrier, inc=1, device_id={"layout": column + 1}, device_id_type=mesh_id
        )

    gathered[0] = jnp.zeros(gathered.shape[1:], jnp.float32)
    for channel in range(own_channels):
        gathered[0, channel * tap_rows : channel * tap_rows + edge, 0:edge] = kernels_ref[
            channel // own_kernels, channel % own_kernels
        ].astype(jnp.float32)
        gathered[0, own_channels * tap_rows + channel, :] = jnp.full(
            (128,), weights_ref[channel % own_kernels], jnp.float32
        )

    tile_edge = cols // occupancy_ref.shape[1]
    lane = lax.broadcasted_iota(jnp.int32, (1, cols), 1)
    live_line = jnp.zeros((1, cols), jnp.float32)
    for tile in range(occupancy_ref.shape[1]):
        inside = jnp.logical_and(lane >= tile * tile_edge, lane < (tile + 1) * tile_edge)
        live_line = jnp.where(inside, occupancy_ref[0, tile].astype(jnp.float32), live_line)

    def mask_of(start, count):
        values = jax.nn.sigmoid(theta_ref[pl.ds(start, count), :].astype(jnp.float32)) * live_line
        return values.astype(jnp.bfloat16)

    def fill_halo(theta_start, target_start):
        halo_out[0:halo_rows, :] = mask_of(theta_start, halo_rows)
        halo_out[halo_rows : halo_rows + margin, :] = target_ref[pl.ds(target_start, margin), :]
        halo_out[halo_rows + margin :, :] = jnp.broadcast_to(live_line, (margin, cols)).astype(
            jnp.bfloat16
        )

    @pl.when(sends_up)
    def _():
        fill_halo(local_rows - halo_rows, local_rows - margin)

    @pl.when(sends_down)
    def _():
        fill_halo(0, 0)

    greeted = (column > 0).astype(jnp.int32) + (column < layouts - 1).astype(jnp.int32)
    pl.semaphore_wait(barrier, sharers - 1 + at_edge.astype(jnp.int32) * greeted)

    def halo_copy(side, neighbour):
        return pltpu.make_async_remote_copy(
            src_ref=halo_out, dst_ref=halo_in.at[side], send_sem=halo_send_sem,
            recv_sem=halo_recv_sem.at[side], device_id={"layout": neighbour},
            device_id_type=mesh_id,
        )

    @pl.when(sends_up)
    def _():
        halo_copy(0, column + 1).start()

    @pl.when(sends_down)
    def _():
        halo_copy(1, column - 1).start()

    tap_copies = [
        pltpu.make_async_remote_copy(
            src_ref=gathered.at[0], dst_ref=gathered.at[offset], send_sem=send_sem.at[offset],
            recv_sem=recv_sem.at[offset],
            device_id={"kernel": lax.rem(sharer + offset, sharers)}, device_id_type=mesh_id,
        )
        for offset in range(1, sharers)
    ]
    for copy in tap_copies:
        copy.start()

    first = pl.multiple_of(sharer * share, 32)
    mask_ref[:, cols:] = jnp.zeros((share + 2 * halo_rows, lanes - cols), jnp.float32)
    mask_ref[halo_rows : halo_rows + share, :cols] = mask_of(first, share).astype(jnp.float32)
    target_near[margin : margin + share, :] = target_ref[pl.ds(first, share), :].astype(
        jnp.float32
    )
    live_near[margin : margin + share, :] = jnp.broadcast_to(live_line, (share, cols))

    def place(mask_at, near_at, mask_values, target_values, live_values):
        mask_ref[mask_at : mask_at + halo_rows, :cols] = mask_values
        target_near[near_at : near_at + margin, :] = target_values
        live_near[near_at : near_at + margin, :] = live_values

    def place_own(mask_at, near_at, mask_start, near_start):
        place(
            mask_at, near_at, mask_of(mask_start, halo_rows).astype(jnp.float32),
            target_ref[pl.ds(near_start, margin), :].astype(jnp.float32),
            jnp.broadcast_to(live_line, (margin, cols)),
        )

    def place_received(mask_at, near_at, side):
        place(
            mask_at, near_at, halo_in[side, 0:halo_rows, :].astype(jnp.float32),
            halo_in[side, halo_rows : halo_rows + margin, :].astype(jnp.float32),
            halo_in[side, halo_rows + margin :, :].astype(jnp.float32),
        )

    def place_nothing(mask_at, near_at):
        place(
            mask_at, near_at, jnp.zeros((halo_rows, cols), jnp.float32),
            jnp.zeros((margin, cols), jnp.float32), jnp.zeros((margin, cols), jnp.float32),
        )

    high_mask, high_near = halo_rows + share, margin + share

    @pl.when(jnp.logical_not(is_first))
    def _():
        place_own(
            0, 0, pl.multiple_of(first - halo_rows, 32), pl.multiple_of(first - margin, 16)
        )

    @pl.when(jnp.logical_not(is_last))
    def _():
        after = pl.multiple_of(first + share, 32)
        place_own(high_mask, high_near, after, after)

    @pl.when(jnp.logical_and(is_first, column == 0))
    def _():
        place_nothing(0, 0)

    @pl.when(jnp.logical_and(is_last, column == layouts - 1))
    def _():
        place_nothing(high_mask, high_near)

    @pl.when(has_low)
    def _():
        halo_copy(0, column - 1).wait_recv()
        place_received(0, 0, 0)

    @pl.when(has_high)
    def _():
        halo_copy(1, column + 1).wait_recv()
        place_received(high_mask, high_near, 1)

    skip = halo_rows - margin - radius
    around = mask_ref[skip : skip + shifted.shape[1], :]
    for tap in range(edge):
        moved = around if tap == radius else pltpu.roll(around, (radius - tap) % lanes, 1)
        shifted[tap] = moved[:, :cols]

    for copy in tap_copies:
        copy.wait()

    taps = gathered[:, 0 : own_channels * tap_rows, :].reshape(channels * tap_rows, 128)
    taps = taps.astype(jnp.bfloat16)
    spread_row = lax.broadcasted_iota(jnp.int32, (128, forward_depth), 0)
    spread_lane = lax.broadcasted_iota(jnp.int32, (128, forward_depth), 1)
    ahead = spread_lane - forward_window * spread_row
    spread = jnp.logical_and(ahead >= 0, ahead < forward_window)
    spread = jnp.where(spread, 1.0, 0.0).astype(jnp.bfloat16)
    wide = jnp.dot(taps, spread, preferred_element_type=jnp.float32)
    wide = wide.reshape(channels, tap_rows, forward_depth)
    line = lax.broadcasted_iota(jnp.int32, (tap_rows, forward_depth), 1)
    down = lax.broadcasted_iota(jnp.int32, (tap_rows, forward_depth), 0)
    chosen = jnp.zeros((tap_rows, forward_depth), jnp.bool_)
    for tap in range(edge):
        chosen = jnp.logical_or(chosen, line - forward_window * tap == down)
    forward_line = jnp.sum(jnp.where(chosen[None], wide, 0.0), axis=1)

    def toeplitz(lines):
        count, depth = lines.shape
        rows = jnp.broadcast_to(lines[:, None, :], (count, step_rows, depth))
        rows = rows.reshape(count * step_rows, depth)
        place_in_step = lax.broadcasted_iota(jnp.int32, rows.shape, 0) & (step_rows - 1)
        bit = 1
        while bit < step_rows:
            rows = jnp.where((place_in_step & bit) != 0, pltpu.roll(rows, bit, 1), rows)
            bit *= 2
        return rows.astype(jnp.bfloat16)

    forward_ref[...] = toeplitz(forward_line)
    extent = (channels, tap_rows, adjoint_depth)
    channel_at = lax.broadcasted_iota(jnp.int32, extent, 0)
    row_at = lax.broadcasted_iota(jnp.int32, extent, 1)
    lane_at = lax.broadcasted_iota(jnp.int32, extent, 2)
    turn = lane_at == channel_at * adjoint_window + (margin + radius) - row_at
    turn = jnp.logical_and(turn, row_at < edge)
    turn = jnp.where(turn, 1.0, 0.0).reshape(channels * tap_rows, adjoint_depth)
    adjoint_line = lax.dot_general(
        taps, turn.astype(jnp.bfloat16), (((0,), (0,)), ((), ())),
        preferred_element_type=jnp.float32,
    )
    adjoint_ref[...] = toeplitz(adjoint_line[:edge])

    def weight_of(channel):
        slot, own = channel // own_channels, channel % own_channels
        at = own_channels * tap_rows + own
        return jnp.broadcast_to(gathered[slot, at : at + 1, 0:1], (step_rows, cols))

    pad_depth = forward_depth - edge * forward_window

    def forward_step(index):
        start = index * step_rows
        windows = shifted[:, pl.ds(start, forward_window), :].reshape(-1, cols)
        windows = jnp.concatenate([windows, jnp.zeros((pad_depth, cols), jnp.float32)], axis=0)
        fields = jnp.dot(
            forward_ref[...], windows.astype(jnp.bfloat16), preferred_element_type=jnp.float32
        ).reshape(channels, step_rows, cols)
        intensity = jnp.zeros((step_rows, cols), jnp.float32)
        for channel in range(channels):
            intensity += weight_of(channel) * (fields[channel] * fields[channel])
        resist = jax.nn.sigmoid(steepness * (intensity - threshold))
        response = 2.0 * steepness * (resist - target_near[pl.ds(start, step_rows), :])
        response = response * resist * (1.0 - resist) * live_near[pl.ds(start, step_rows), :]
        for channel in range(channels):
            factor = 2.0 * weight_of(channel) * response
            products[channel, pl.ds(start, step_rows), :] = (factor * fields[channel]).astype(
                jnp.bfloat16
            )

    def adjoint_step(index):
        start = index * step_rows
        windows = products[:, pl.ds(start, adjoint_window), :].reshape(-1, cols)
        terms = jnp.dot(adjoint_ref[...], windows, preferred_element_type=jnp.float32)
        beside = jnp.zeros((step_rows, lanes - cols), jnp.float32)
        total = terms[radius * step_rows : (radius + 1) * step_rows, :]
        for tap in range(edge):
            if tap != radius:
                term = terms[tap * step_rows : (tap + 1) * step_rows, :]
                term = jnp.concatenate([term, beside], axis=1)
                total = total + pltpu.roll(term, (tap - radius) % lanes, 1)[:, :cols]
        out_ref[pl.ds(start, step_rows), :] = total * live_line

    for index in range((share + 2 * margin) // step_rows):
        forward_step(index)
    for index in range(share // step_rows):
        adjoint_step(index)

    @pl.when(sends_up)
    def _():
        halo_copy(0, column + 1).wait_send()

    @pl.when(sends_down)
    def _():
        halo_copy(1, column - 1).wait_send()


def on_device(theta, target, occupancy, kernels, kernel_weights):
    local_rows, cols = theta.shape
    layouts, sharers = lax.axis_size("layout"), lax.axis_size("kernel")
    own_channels = kernels.shape[0] * kernels.shape[1]
    channels = own_channels * sharers
    edge = kernels.shape[-1]
    share = local_rows // sharers
    lanes = cols + 128
    forward_window = -(-(step_rows + edge - 1) // 8) * 8
    forward_depth = -(-edge * forward_window // 128) * 128
    adjoint_window = step_rows + 2 * margin
    near_rows = share + 2 * margin
    vmem, smem = pltpu.VMEM, pltpu.SMEM
    return pl.pallas_call(
        functools.partial(band_kernel, layouts, sharers),
        out_shape=jax.ShapeDtypeStruct((share, cols), jnp.float32),
        in_specs=[
            pl.BlockSpec(memory_space=vmem),
            pl.BlockSpec(memory_space=vmem),
            pl.BlockSpec(memory_space=smem),
            pl.BlockSpec(memory_space=vmem),
            pl.BlockSpec(memory_space=smem),
        ],
        out_specs=pl.BlockSpec(memory_space=vmem),
        scratch_shapes=[
            vmem((sharers, own_channels * tap_rows + 8, 128), jnp.float32),
            vmem((halo_rows + 2 * margin, cols), jnp.bfloat16),
            vmem((2, halo_rows + 2 * margin, cols), jnp.bfloat16),
            vmem((share + 2 * halo_rows, lanes), jnp.float32),
            vmem((near_rows, cols), jnp.float32),
            vmem((near_rows, cols), jnp.float32),
            vmem((edge, near_rows - step_rows + forward_window, cols), jnp.float32),
            vmem((channels, near_rows, cols), jnp.bfloat16),
            vmem((channels * step_rows, forward_depth), jnp.bfloat16),
            vmem((edge * step_rows, channels * adjoint_window), jnp.bfloat16),
            pltpu.SemaphoreType.DMA((sharers,)),
            pltpu.SemaphoreType.DMA((sharers,)),
            pltpu.SemaphoreType.DMA,
            pltpu.SemaphoreType.DMA((2,)),
        ],
        compiler_params=pltpu.CompilerParams(
            collective_id=0, has_side_effects=True, vmem_limit_bytes=48 * 1024 * 1024
        ),
    )(theta, target, occupancy, kernels, kernel_weights)


def solution(mesh):
    placed = (
        P(("group", "layout"), None),
        P(("group", "layout"), None),
        P(("group", "layout"), None),
        P(None, "kernel", None, None),
        P("kernel"),
    )
    return jax.shard_map(
        on_device,
        mesh=mesh,
        in_specs=placed,
        out_specs=P(("group", "layout", "kernel"), None),
        check_vma=False,
    )
```

profile of v0, /device:TPU:1, one launch (start us, length us, event | category | flops | bytes accessed | tf_op | source)
XLA Modules:
  0.0 14.0 jit_solution(1090593798048215002)
XLA Ops:
  0.0 0.0 copy-start.3
  0.0 0.0 copy-start.2
  0.0 0.8 %copy.6.kernels_ref = bf16[2,2,19,19]{3,2,1,0:T(8,128)(2,1)S(1)} copy(bf16[2,2,19,19]{3,1,2,0:T(2,128)(2,1)} %param.8) | data formatting | bytes 5776 | tf_op args[3]
  0.8 0.0 copy-done.3
  0.8 0.0 copy-done.2
  0.8 0.0 copy-start
  0.8 0.9 %copy-done = bf16[256,512]{1,0:T(8,128)(2,1)S(1)} copy-done((bf16[256,512]{1,0:T(8,128)(2,1)S(1)}, bf16[256,512]{1,0:T(8,128)(2,1)}, u32[]{:S(2)}) %copy-start) | copy-done | bytes 262168
  1.7 0.0 copy-start.1
  1.7 0.9 %copy-done.1 = bf16[256,512]{1,0:T(8,128)(2,1)S(1)} copy-done((bf16[256,512]{1,0:T(8,128)(2,1)S(1)}, bf16[256,512]{1,0:T(8,128)(2,1)}, u32[]{:S(2)}) %copy-start.1) | copy-done | bytes 262168
  2.7 10.7 %shard_map.55 = f32[64,512]{1,0:T(8,128)S(1)} custom-call(bf16[256,512]{1,0:T(8,128)(2,1)S(1)} %copy-done, bf16[256,512]{1,0:T(8,128)(2,1)S(1)} %copy-done.1, s32[1,2]{1,0:T(1,128)S(1)} %copy-done.2, bf16[2,2,19,19]{3,2,1,0:T(8,128)(2,1)S(1)} %copy.6.kernels_ref, f32[2]{0:T(128)S(1)} %copy-done.3), custom_call_target="tpu_custom_call" | custom-call | tf_op jit(solution)/shard_map/pallas_call | solution.py:307
  13.3 0.7 %copy.8 = f32[64,512]{1,0:T(8,128)} copy(f32[64,512]{1,0:T(8,128)S(1)} %shard_map.55) | data formatting | bytes 262144
Async XLA Ops:
  0.0 0.8 %copy-start.3 = (f32[2]{0:T(128)S(1)}, f32[2]{0:T(128)}, u32[]{:S(2)}) copy-start(f32[2]{0:T(128)} %weights_ref.1) | copy-start | bytes 28
  0.0 0.8 %copy-start.2 = (s32[1,2]{1,0:T(1,128)S(1)}, s32[1,2]{1,0:T(1,128)}, u32[]{:S(2)}) copy-start(s32[1,2]{1,0:T(1,128)} %occupancy_ref.1) | copy-start | bytes 28
  0.8 1.0 %copy-start = (bf16[256,512]{1,0:T(8,128)(2,1)S(1)}, bf16[256,512]{1,0:T(8,128)(2,1)}, u32[]{:S(2)}) copy-start(bf16[256,512]{1,0:T(8,128)(2,1)} %theta_ref.1) | copy-start | bytes 786436
  1.7 0.9 %copy-start.1 = (bf16[256,512]{1,0:T(8,128)(2,1)S(1)}, bf16[256,512]{1,0:T(8,128)(2,1)}, u32[]{:S(2)}) copy-start(bf16[256,512]{1,0:T(8,128)(2,1)} %target_ref.1) | copy-start | bytes 786436
where the time goes:
time: 14.2 us; the launch traced here: 14 us
  Pallas kernels  10.7 us (75%)
  local copies, waits for them, and re-layouts  3.32 us (23%)
    pallas_call x1, Pallas kernels, on_device(): pl.pallas_call(functools.partial(band_kernel, layouts, sharers), out_shap...  10.7 us
    unnamed x10, local copies, waits for them, and re-layouts  3.32 us

commit v1 on v0

--- a/solution.py
+++ b/solution.py
@@ -12,16 +12,17 @@
 margin = 16
 halo_rows = 32
 tap_rows = 24
+tap_lanes = 32
 mesh_id = pl.DeviceIdType.MESH
 
 
 def band_kernel(
-    layouts, sharers, theta_ref, target_ref, occupancy_ref, kernels_ref, weights_ref, out_ref,
-    gathered, halo_out, halo_in, mask_ref, target_near, live_near, shifted, products, forward_ref,
+    layouts, sharers, theta_hbm, target_hbm, occupancy_hbm, kernels_hbm, weights_hbm, out_ref,
+    theta_ref, target_ref, occupancy_ref, kernels_ref, weights_ref, load_sem, gathered, halo_out, halo_in, mask_ref, target_near, live_near, shifted, products, forward_ref,
     adjoint_ref, send_sem, recv_sem, halo_send_sem, halo_recv_sem,
 ):
     local_rows, cols = theta_ref.shape
-    parts, own_kernels, edge, _ = kernels_ref.shape
+    parts, edge, own_kernels, _ = kernels_ref.shape
     own_channels = parts * own_kernels
     channels = own_channels * sharers
     radius = edge // 2
@@ -41,6 +42,16 @@
     sends_down = jnp.logical_and(is_last, column > 0)
     at_edge = jnp.logical_or(is_first, is_last)
 
+    loads = [
+        pltpu.make_async_copy(source, place, load_sem.at[index])
+        for index, (source, place) in enumerate((
+            (kernels_hbm, kernels_ref), (weights_hbm, weights_ref),
+            (occupancy_hbm, occupancy_ref), (theta_hbm, theta_ref), (target_hbm, target_ref),
+        ))
+    ]
+    for load in loads:
+        load.start()
+
     barrier = pltpu.get_barrier_semaphore()
     for offset in range(1, sharers):
         pl.semaphore_signal(
@@ -61,20 +72,26 @@
         )
 
     gathered[0] = jnp.zeros(gathered.shape[1:], jnp.float32)
+    loads[0].wait()
+    loads[1].wait()
     for channel in range(own_channels):
-        gathered[0, channel * tap_rows : channel * tap_rows + edge, 0:edge] = kernels_ref[
-            channel // own_kernels, channel % own_kernels
-        ].astype(jnp.float32)
-        gathered[0, own_channels * tap_rows + channel, :] = jnp.full(
-            (128,), weights_ref[channel % own_kernels], jnp.float32
-        )
+        part, own = channel // own_kernels, channel % own_kernels
+        lane_start = channel * tap_lanes
+        taps = kernels_ref[part].astype(jnp.float32)
+        for tap in range(edge):
+            gathered[0, tap : tap + 1, lane_start : lane_start + edge] = taps[tap, own : own + 1]
+        gathered[0, edge : edge + 1, lane_start : lane_start + edge] = jnp.broadcast_to(
+            weights_ref[0:1, own : own + 1], (1, edge)
+        )
+    for load in loads[2:]:
+        load.wait()
 
     tile_edge = cols // occupancy_ref.shape[1]
     lane = lax.broadcasted_iota(jnp.int32, (1, cols), 1)
     live_line = jnp.zeros((1, cols), jnp.float32)
     for tile in range(occupancy_ref.shape[1]):
         inside = jnp.logical_and(lane >= tile * tile_edge, lane < (tile + 1) * tile_edge)
-        live_line = jnp.where(inside, occupancy_ref[0, tile].astype(jnp.float32), live_line)
+        live_line = jnp.where(inside, occupancy_ref[0:1, tile : tile + 1].astype(jnp.float32), live_line)
 
     def mask_of(start, count):
         values = jax.nn.sigmoid(theta_ref[pl.ds(start, count), :].astype(jnp.float32)) * live_line
@@ -178,6 +195,29 @@
     def _():
         place_nothing(high_mask, high_near)
 
+    spread_row = lax.broadcasted_iota(jnp.int32, (128, forward_depth), 0)
+    spread_lane = lax.broadcasted_iota(jnp.int32, (128, forward_depth), 1)
+    spreads = []
+    for channel in range(own_channels):
+        ahead = spread_lane - forward_window * (spread_row - channel * tap_lanes)
+        spread = jnp.logical_and(ahead >= 0, ahead < forward_window)
+        spreads.append(jnp.where(spread, 1.0, 0.0).astype(jnp.bfloat16))
+    line = lax.broadcasted_iota(jnp.int32, (tap_rows, forward_depth), 1)
+    down = lax.broadcasted_iota(jnp.int32, (tap_rows, forward_depth), 0)
+    chosen = jnp.zeros((tap_rows, forward_depth), jnp.float32)
+    for tap in range(edge):
+        chosen = jnp.where(line - forward_window * tap == down, 1.0, chosen)
+    chosen = jnp.where(down < edge, chosen, 0.0)
+    group_depth = sharers * adjoint_window
+    turn_lanes = -(-group_depth // 128) * 128
+    extent = (sharers, tap_rows, turn_lanes)
+    slot_at = lax.broadcasted_iota(jnp.int32, extent, 0)
+    row_at = lax.broadcasted_iota(jnp.int32, extent, 1)
+    lane_at = lax.broadcasted_iota(jnp.int32, extent, 2)
+    turn = lane_at == slot_at * adjoint_window + (margin + radius) - row_at
+    turn = jnp.logical_and(turn, row_at < edge)
+    turn = jnp.where(turn, 1.0, 0.0).reshape(sharers * tap_rows, turn_lanes).astype(jnp.bfloat16)
+
     @pl.when(has_low)
     def _():
         halo_copy(0, column - 1).wait_recv()
@@ -197,21 +237,13 @@
     for copy in tap_copies:
         copy.wait()
 
-    taps = gathered[:, 0 : own_channels * tap_rows, :].reshape(channels * tap_rows, 128)
-    taps = taps.astype(jnp.bfloat16)
-    spread_row = lax.broadcasted_iota(jnp.int32, (128, forward_depth), 0)
-    spread_lane = lax.broadcasted_iota(jnp.int32, (128, forward_depth), 1)
-    ahead = spread_lane - forward_window * spread_row
-    spread = jnp.logical_and(ahead >= 0, ahead < forward_window)
-    spread = jnp.where(spread, 1.0, 0.0).astype(jnp.bfloat16)
-    wide = jnp.dot(taps, spread, preferred_element_type=jnp.float32)
-    wide = wide.reshape(channels, tap_rows, forward_depth)
-    line = lax.broadcasted_iota(jnp.int32, (tap_rows, forward_depth), 1)
-    down = lax.broadcasted_iota(jnp.int32, (tap_rows, forward_depth), 0)
-    chosen = jnp.zeros((tap_rows, forward_depth), jnp.bool_)
-    for tap in range(edge):
-        chosen = jnp.logical_or(chosen, line - forward_window * tap == down)
-    forward_line = jnp.sum(jnp.where(chosen[None], wide, 0.0), axis=1)
+    taps = gathered[...].reshape(sharers * tap_rows, 128).astype(jnp.bfloat16)
+    lines = []
+    for spread in spreads:
+        wide = jnp.dot(taps, spread, preferred_element_type=jnp.float32)
+        wide = wide.reshape(sharers, tap_rows, forward_depth)
+        lines.append(jnp.sum(wide * chosen[None], axis=1))
+    forward_line = jnp.concatenate(lines, axis=0)
 
     def toeplitz(lines):
         count, depth = lines.shape
@@ -225,23 +257,25 @@
         return rows.astype(jnp.bfloat16)
 
     forward_ref[...] = toeplitz(forward_line)
-    extent = (channels, tap_rows, adjoint_depth)
-    channel_at = lax.broadcasted_iota(jnp.int32, extent, 0)
-    row_at = lax.broadcasted_iota(jnp.int32, extent, 1)
-    lane_at = lax.broadcasted_iota(jnp.int32, extent, 2)
-    turn = lane_at == channel_at * adjoint_window + (margin + radius) - row_at
-    turn = jnp.logical_and(turn, row_at < edge)
-    turn = jnp.where(turn, 1.0, 0.0).reshape(channels * tap_rows, adjoint_depth)
-    adjoint_line = lax.dot_general(
-        taps, turn.astype(jnp.bfloat16), (((0,), (0,)), ((), ())),
-        preferred_element_type=jnp.float32,
+    turned = lax.dot_general(
+        taps, turn, (((0,), (0,)), ((), ())), preferred_element_type=jnp.float32
     )
+    rest = jnp.zeros((tap_rows, adjoint_depth - turn_lanes), jnp.float32)
+    adjoint_line = None
+    for channel in range(own_channels):
+        piece = turned[channel * tap_lanes : channel * tap_lanes + tap_rows]
+        piece = jnp.concatenate([piece, rest], axis=1)
+        if channel:
+            piece = pltpu.roll(piece, channel * group_depth, 1)
+        adjoint_line = piece if adjoint_line is None else adjoint_line + piece
     adjoint_ref[...] = toeplitz(adjoint_line[:edge])
 
     def weight_of(channel):
-        slot, own = channel // own_channels, channel % own_channels
-        at = own_channels * tap_rows + own
-        return jnp.broadcast_to(gathered[slot, at : at + 1, 0:1], (step_rows, cols))
+        own, slot = channel // sharers, channel % sharers
+        lane_start = own * tap_lanes
+        return jnp.broadcast_to(
+            gathered[slot, edge : edge + 1, lane_start : lane_start + 1], (step_rows, cols)
+        )
 
     pad_depth = forward_depth - edge * forward_window
 
@@ -303,20 +337,22 @@
     forward_depth = -(-edge * forward_window // 128) * 128
     adjoint_window = step_rows + 2 * margin
     near_rows = share + 2 * margin
-    vmem, smem = pltpu.VMEM, pltpu.SMEM
+    vmem = pltpu.VMEM
+    kernels = jnp.transpose(kernels, (0, 2, 1, 3))
+    weights = kernel_weights.reshape(1, -1)
     return pl.pallas_call(
         functools.partial(band_kernel, layouts, sharers),
         out_shape=jax.ShapeDtypeStruct((share, cols), jnp.float32),
-        in_specs=[
-            pl.BlockSpec(memory_space=vmem),
-            pl.BlockSpec(memory_space=vmem),
-            pl.BlockSpec(memory_space=smem),
-            pl.BlockSpec(memory_space=vmem),
-            pl.BlockSpec(memory_space=smem),
-        ],
+        in_specs=[pl.BlockSpec(memory_space=pltpu.HBM)] * 5,
         out_specs=pl.BlockSpec(memory_space=vmem),
         scratch_shapes=[
-            vmem((sharers, own_channels * tap_rows + 8, 128), jnp.float32),
+            vmem(theta.shape, theta.dtype),
+            vmem(target.shape, target.dtype),
+            vmem(occupancy.shape, occupancy.dtype),
+            vmem(kernels.shape, kernels.dtype),
+            vmem(weights.shape, weights.dtype),
+            pltpu.SemaphoreType.DMA((5,)),
+            vmem((sharers, tap_rows, 128), jnp.float32),
             vmem((halo_rows + 2 * margin, cols), jnp.bfloat16),
             vmem((2, halo_rows + 2 * margin, cols), jnp.bfloat16),
             vmem((share + 2 * halo_rows, lanes), jnp.float32),
@@ -332,9 +368,9 @@
             pltpu.SemaphoreType.DMA((2,)),
         ],
         compiler_params=pltpu.CompilerParams(
-            collective_id=0, has_side_effects=True, vmem_limit_bytes=48 * 1024 * 1024
+            collective_id=0, has_side_effects=True, vmem_limit_bytes=64 * 1024 * 1024 - 192 * 1024
         ),
-    )(theta, target, occupancy, kernels, kernel_weights)
+    )(theta, target, occupancy, kernels, weights)
 
 
 def solution(mesh):

time: 14.2 us -> 12.2 us (0.86)
  the two profiles are of different devices: /device:TPU:1 before, /device:TPU:0 now
where the time goes in v1:
time: 12.2 us; the launch traced here: 12 us
  Pallas kernels  10.4 us (85%)
  local copies, waits for them, and re-layouts  1.57 us (13%)
    pallas_call x1, Pallas kernels, on_device(): pl.pallas_call(functools.partial(band_kernel, layouts, sharers), out_shap...  10.4 us
    unnamed x1, local copies, waits for them, and re-layouts  1.57 us

profile of v1, /device:TPU:0, one launch (start us, length us, event | category | flops | bytes accessed | tf_op | source)
XLA Modules:
  0.0 12.0 jit_solution(10687398662304273451)
XLA Ops:
  0.0 10.4 %shard_map.55 = f32[64,512]{1,0:T(8,128)} custom-call(bf16[256,512]{1,0:T(8,128)(2,1)} %theta_hbm.1, bf16[256,512]{1,0:T(8,128)(2,1)} %target_hbm.1, s32[1,2]{1,0:T(1,128)} %occupancy_hbm.1, bf16[2,19,2,19]{3,2,1,0:T(2,128)(2,1)} %bitcast.2, f32[1,2]{1,0:T(1,128)} %bitcast.3), custom_call_target="tpu_custom_call" | custom-call | tf_op jit(solution)/shard_map/pallas_call | solution.py:343
  10.4 1.6 %copy.7 = f32[64,512]{1,0:T(8,128)} copy(f32[64,512]{1,0:T(8,128)} %shard_map.55) | data formatting | bytes 262144

commit v2 on v1

--- a/solution.py
+++ b/solution.py
@@ -368,9 +368,9 @@
             pltpu.SemaphoreType.DMA((2,)),
         ],
         compiler_params=pltpu.CompilerParams(
-            collective_id=0, has_side_effects=True, vmem_limit_bytes=64 * 1024 * 1024 - 192 * 1024
+            collective_id=0, has_side_effects=True, vmem_limit_bytes=48 * 1024 * 1024
         ),
-    )(theta, target, occupancy, kernels, weights)
+    )(*(pltpu.with_memory_space_constraint(x, pltpu.HBM) for x in (theta, target, occupancy, kernels, weights)))
 
 
 def solution(mesh):

time: 12.2 us -> 10.6 us (0.87)
  local copies, waits for them, and re-layouts: 1.57 us -> 0.66 us
  Pallas kernels: 10.4 us -> 9.79 us
    unnamed x1, local copies, waits for them, and re-layouts: 1.57 us -> 0.66 us
    pallas_call x1, Pallas kernels: 10.4 us -> 9.79 us  [on_device(): pl.pallas_call(functools.partial(band_kernel, layouts, sharers), out_shap...]
where the time goes in v2:
time: 10.6 us; the launch traced here: 10.5 us
  Pallas kernels  9.79 us (92%)
  local copies, waits for them, and re-layouts  0.66 us (6%)
    pallas_call x1, Pallas kernels, on_device(): pl.pallas_call(functools.partial(band_kernel, layouts, sharers), out_shap...  9.79 us
    unnamed x1, local copies, waits for them, and re-layouts  0.66 us

profile of v2, /device:TPU:0, one launch (start us, length us, event | category | flops | bytes accessed | tf_op | source)
XLA Modules:
  0.0 10.5 jit_solution(363831732792337813)
XLA Ops:
  0.0 9.8 %shard_map.55 = f32[64,512]{1,0:T(8,128)S(1)} custom-call(bf16[256,512]{1,0:T(8,128)(2,1)} %theta_hbm.1, bf16[256,512]{1,0:T(8,128)(2,1)} %target_hbm.1, s32[1,2]{1,0:T(1,128)} %occupancy_hbm.1, bf16[2,19,2,19]{3,2,1,0:T(2,128)(2,1)} %bitcast.2, f32[1,2]{1,0:T(1,128)} %bitcast.3), custom_call_target="tpu_custom_call" | custom-call | tf_op jit(solution)/shard_map/pallas_call | solution.py:343
  9.8 0.7 %copy.7 = f32[64,512]{1,0:T(8,128)} copy(f32[64,512]{1,0:T(8,128)S(1)} %shard_map.55) | data formatting | bytes 262144

commit v3 on v2

--- a/solution.py
+++ b/solution.py
@@ -83,6 +83,20 @@
         gathered[0, edge : edge + 1, lane_start : lane_start + edge] = jnp.broadcast_to(
             weights_ref[0:1, own : own + 1], (1, edge)
         )
+    greeted = (column > 0).astype(jnp.int32) + (column < layouts - 1).astype(jnp.int32)
+    pl.semaphore_wait(barrier, sharers - 1 + at_edge.astype(jnp.int32) * greeted)
+
+    tap_copies = [
+        pltpu.make_async_remote_copy(
+            src_ref=gathered.at[0], dst_ref=gathered.at[offset], send_sem=send_sem.at[offset],
+            recv_sem=recv_sem.at[offset],
+            device_id={"kernel": lax.rem(sharer + offset, sharers)}, device_id_type=mesh_id,
+        )
+        for offset in range(1, sharers)
+    ]
+    for copy in tap_copies:
+        copy.start()
+
     for load in loads[2:]:
         load.wait()
 
@@ -112,9 +126,6 @@
     def _():
         fill_halo(0, 0)
 
-    greeted = (column > 0).astype(jnp.int32) + (column < layouts - 1).astype(jnp.int32)
-    pl.semaphore_wait(barrier, sharers - 1 + at_edge.astype(jnp.int32) * greeted)
-
     def halo_copy(side, neighbour):
         return pltpu.make_async_remote_copy(
             src_ref=halo_out, dst_ref=halo_in.at[side], send_sem=halo_send_sem,
@@ -129,17 +140,6 @@
     @pl.when(sends_down)
     def _():
         halo_copy(1, column - 1).start()
-
-    tap_copies = [
-        pltpu.make_async_remote_copy(
-            src_ref=gathered.at[0], dst_ref=gathered.at[offset], send_sem=send_sem.at[offset],
-            recv_sem=recv_sem.at[offset],
-            device_id={"kernel": lax.rem(sharer + offset, sharers)}, device_id_type=mesh_id,
-        )
-        for offset in range(1, sharers)
-    ]
-    for copy in tap_copies:
-        copy.start()
 
     first = pl.multiple_of(sharer * share, 32)
     mask_ref[:, cols:] = jnp.zeros((share + 2 * halo_rows, lanes - cols), jnp.float32)
@@ -247,13 +247,16 @@
 
     def toeplitz(lines):
         count, depth = lines.shape
-        rows = jnp.broadcast_to(lines[:, None, :], (count, step_rows, depth))
-        rows = rows.reshape(count * step_rows, depth)
-        place_in_step = lax.broadcasted_iota(jnp.int32, rows.shape, 0) & (step_rows - 1)
-        bit = 1
-        while bit < step_rows:
-            rows = jnp.where((place_in_step & bit) != 0, pltpu.roll(rows, bit, 1), rows)
-            bit *= 2
+        rows = jnp.concatenate(
+            [
+                pltpu.roll(
+                    jnp.broadcast_to(lines[row : row + 1], (step_rows, depth)), 0, 1, stride=1,
+                    stride_axis=0,
+                )
+                for row in range(count)
+            ],
+            axis=0,
+        )
         return rows.astype(jnp.bfloat16)
 
     forward_ref[...] = toeplitz(forward_line)

time: 10.6 us -> 9.47 us (0.89)
  Pallas kernels: 9.79 us -> 8.66 us
    pallas_call x1, Pallas kernels: 9.79 us -> 8.66 us  [on_device(): pl.pallas_call(functools.partial(band_kernel, layouts, sharers), out_shap...]
where the time goes in v3:
time: 9.47 us; the launch traced here: 9.33 us
  Pallas kernels  8.66 us (91%)
  local copies, waits for them, and re-layouts  0.66 us (7%)
    pallas_call x1, Pallas kernels, on_device(): pl.pallas_call(functools.partial(band_kernel, layouts, sharers), out_shap...  8.66 us
    unnamed x1, local copies, waits for them, and re-layouts  0.66 us

profile of v3, /device:TPU:0, one launch (start us, length us, event | category | flops | bytes accessed | tf_op | source)
XLA Modules:
  0.0 9.3 jit_solution(15831999673170729495)
XLA Ops:
  0.0 8.7 %shard_map.55 = f32[64,512]{1,0:T(8,128)S(1)} custom-call(bf16[256,512]{1,0:T(8,128)(2,1)} %theta_hbm.1, bf16[256,512]{1,0:T(8,128)(2,1)} %target_hbm.1, s32[1,2]{1,0:T(1,128)} %occupancy_hbm.1, bf16[2,19,2,19]{3,2,1,0:T(2,128)(2,1)} %bitcast.2, f32[1,2]{1,0:T(1,128)} %bitcast.3), custom_call_target="tpu_custom_call" | custom-call | tf_op jit(solution)/shard_map/pallas_call | solution.py:346
  8.7 0.7 %copy.7 = f32[64,512]{1,0:T(8,128)} copy(f32[64,512]{1,0:T(8,128)S(1)} %shard_map.55) | data formatting | bytes 262144

commit v4 on v3

--- a/solution.py
+++ b/solution.py
@@ -260,18 +260,6 @@
         return rows.astype(jnp.bfloat16)
 
     forward_ref[...] = toeplitz(forward_line)
-    turned = lax.dot_general(
-        taps, turn, (((0,), (0,)), ((), ())), preferred_element_type=jnp.float32
-    )
-    rest = jnp.zeros((tap_rows, adjoint_depth - turn_lanes), jnp.float32)
-    adjoint_line = None
-    for channel in range(own_channels):
-        piece = turned[channel * tap_lanes : channel * tap_lanes + tap_rows]
-        piece = jnp.concatenate([piece, rest], axis=1)
-        if channel:
-            piece = pltpu.roll(piece, channel * group_depth, 1)
-        adjoint_line = piece if adjoint_line is None else adjoint_line + piece
-    adjoint_ref[...] = toeplitz(adjoint_line[:edge])
 
     def weight_of(channel):
         own, slot = channel // sharers, channel % sharers
@@ -301,6 +289,20 @@
                 jnp.bfloat16
             )
 
+    def build_adjoint():
+        turned = lax.dot_general(
+            taps, turn, (((0,), (0,)), ((), ())), preferred_element_type=jnp.float32
+        )
+        rest = jnp.zeros((tap_rows, adjoint_depth - turn_lanes), jnp.float32)
+        adjoint_line = None
+        for channel in range(own_channels):
+            piece = turned[channel * tap_lanes : channel * tap_lanes + tap_rows]
+            piece = jnp.concatenate([piece, rest], axis=1)
+            if channel:
+                piece = pltpu.roll(piece, channel * group_depth, 1)
+            adjoint_line = piece if adjoint_line is None else adjoint_line + piece
+        adjoint_ref[...] = toeplitz(adjoint_line[:edge])
+
     def adjoint_step(index):
         start = index * step_rows
         windows = products[:, pl.ds(start, adjoint_window), :].reshape(-1, cols)
@@ -314,10 +316,15 @@
                 total = total + pltpu.roll(term, (tap - radius) % lanes, 1)[:, :cols]
         out_ref[pl.ds(start, step_rows), :] = total * live_line
 
-    for index in range((share + 2 * margin) // step_rows):
+    lead = 2 * margin // step_rows
+    for index in range(lead):
         forward_step(index)
+    build_adjoint()
     for index in range(share // step_rows):
-        adjoint_step(index)
+        forward_step(index + lead)
+        if index:
+            adjoint_step(index - 1)
+    adjoint_step(share // step_rows - 1)
 
     @pl.when(sends_up)
     def _():

time: 9.47 us -> 9.48 us (level)
  no operation moved by 1% of the time
where the time goes in v4:
time: 9.48 us; the launch traced here: 9.34 us
  Pallas kernels  8.67 us (91%)
  local copies, waits for them, and re-layouts  0.66 us (7%)
    pallas_call x1, Pallas kernels, on_device(): pl.pallas_call(functools.partial(band_kernel, layouts, sharers), out_shap...  8.67 us
    unnamed x1, local copies, waits for them, and re-layouts  0.66 us

profile of v4, /device:TPU:0, one launch (start us, length us, event | category | flops | bytes accessed | tf_op | source)
XLA Modules:
  0.0 9.3 jit_solution(6966326106702835531)
XLA Ops:
  0.0 8.7 %shard_map.55 = f32[64,512]{1,0:T(8,128)S(1)} custom-call(bf16[256,512]{1,0:T(8,128)(2,1)} %theta_hbm.1, bf16[256,512]{1,0:T(8,128)(2,1)} %target_hbm.1, s32[1,2]{1,0:T(1,128)} %occupancy_hbm.1, bf16[2,19,2,19]{3,2,1,0:T(2,128)(2,1)} %bitcast.2, f32[1,2]{1,0:T(1,128)} %bitcast.3), custom_call_target="tpu_custom_call" | custom-call | tf_op jit(solution)/shard_map/pallas_call | solution.py:353
  8.7 0.7 %copy.7 = f32[64,512]{1,0:T(8,128)} copy(f32[64,512]{1,0:T(8,128)S(1)} %shard_map.55) | data formatting | bytes 262144

commit v5 on v4

--- a/solution.py
+++ b/solution.py
@@ -18,7 +18,7 @@
 
 def band_kernel(
     layouts, sharers, theta_hbm, target_hbm, occupancy_hbm, kernels_hbm, weights_hbm, out_ref,
-    theta_ref, target_ref, occupancy_ref, kernels_ref, weights_ref, load_sem, gathered, halo_out, halo_in, mask_ref, target_near, live_near, shifted, products, forward_ref,
+    theta_ref, target_ref, occupancy_ref, kernels_ref, weights_ref, load_sem, gathered, halo_out, halo_in, mask_ref, target_near, live_near, shifted, windows_ref, products, forward_ref,
     adjoint_ref, send_sem, recv_sem, halo_send_sem, halo_recv_sem,
 ):
     local_rows, cols = theta_ref.shape
@@ -233,6 +233,12 @@
     for tap in range(edge):
         moved = around if tap == radius else pltpu.roll(around, (radius - tap) % lanes, 1)
         shifted[tap] = moved[:, :cols]
+    pad_depth = forward_depth - edge * forward_window
+    for index in range(windows_ref.shape[0]):
+        start = index * step_rows
+        windows = shifted[:, start : start + forward_window, :].reshape(-1, cols)
+        windows = jnp.concatenate([windows, jnp.zeros((pad_depth, cols), jnp.float32)], axis=0)
+        windows_ref[index] = windows.astype(jnp.bfloat16)
 
     for copy in tap_copies:
         copy.wait()
@@ -268,14 +274,10 @@
             gathered[slot, edge : edge + 1, lane_start : lane_start + 1], (step_rows, cols)
         )
 
-    pad_depth = forward_depth - edge * forward_window
-
     def forward_step(index):
         start = index * step_rows
-        windows = shifted[:, pl.ds(start, forward_window), :].reshape(-1, cols)
-        windows = jnp.concatenate([windows, jnp.zeros((pad_depth, cols), jnp.float32)], axis=0)
         fields = jnp.dot(
-            forward_ref[...], windows.astype(jnp.bfloat16), preferred_element_type=jnp.float32
+            forward_ref[...], windows_ref[index], preferred_element_type=jnp.float32
         ).reshape(channels, step_rows, cols)
         intensity = jnp.zeros((step_rows, cols), jnp.float32)
         for channel in range(channels):
@@ -369,6 +371,7 @@
             vmem((near_rows, cols), jnp.float32),
             vmem((near_rows, cols), jnp.float32),
             vmem((edge, near_rows - step_rows + forward_window, cols), jnp.float32),
+            vmem((near_rows // step_rows, forward_depth, cols), jnp.bfloat16),
             vmem((channels, near_rows, cols), jnp.bfloat16),
             vmem((channels * step_rows, forward_depth), jnp.bfloat16),
             vmem((edge * step_rows, channels * adjoint_window), jnp.bfloat16),

time: 9.48 us -> 9.47 us (level)
  no operation moved by 1% of the time
where the time goes in v5:
time: 9.47 us; the launch traced here: 9.33 us
  Pallas kernels  8.66 us (91%)
  local copies, waits for them, and re-layouts  0.66 us (7%)
    pallas_call x1, Pallas kernels, on_device(): pl.pallas_call(functools.partial(band_kernel, layouts, sharers), out_shap...  8.66 us
    unnamed x1, local copies, waits for them, and re-layouts  0.66 us

profile of v5, /device:TPU:0, one launch (start us, length us, event | category | flops | bytes accessed | tf_op | source)
XLA Modules:
  0.0 9.3 jit_solution(965858696310072658)
XLA Ops:
  0.0 8.7 %shard_map.55 = f32[64,512]{1,0:T(8,128)S(1)} custom-call(bf16[256,512]{1,0:T(8,128)(2,1)} %theta_hbm.1, bf16[256,512]{1,0:T(8,128)(2,1)} %target_hbm.1, s32[1,2]{1,0:T(1,128)} %occupancy_hbm.1, bf16[2,19,2,19]{3,2,1,0:T(2,128)(2,1)} %bitcast.2, f32[1,2]{1,0:T(1,128)} %bitcast.3), custom_call_target="tpu_custom_call" | custom-call | tf_op jit(solution)/shard_map/pallas_call | solution.py:355
  8.7 0.7 %copy.7 = f32[64,512]{1,0:T(8,128)} copy(f32[64,512]{1,0:T(8,128)S(1)} %shard_map.55) | data formatting | bytes 262144
